TPU v7x, 128 devices: a whole 4x4x4 slice. The times are simulated.
128 devices in a mesh: dp: 2 (over core), seq: 64 (over x, z, y).
Axes of the slice: x: 4, y: 4, z: 4, core: 2. Of those that a mesh axis runs over, the one named last changes fastest.
Arguments:
- queries: bfloat16 [2, 32768, 1024], P('dp', 'seq'), may hold values from -16 to 16
- keys: bfloat16 [2, 32768, 1024], P('dp', 'seq'), may hold values from -16 to 16
- values: bfloat16 [2, 32768, 1024], P('dp', 'seq'), may hold values from -6 to 6
- offsets: int32 [8], replicated, may hold values from 0 to 15, as said below
- out_weight: bfloat16 [1024, 2048], replicated, may hold values from -0.1875 to 0.1875
- grad_out: bfloat16 [2, 32768, 2048], P('dp', 'seq'), may hold values from -16 to 16
Outputs:
- result: bfloat16 [2, 32768, 2048], P('dp', 'seq')
- grad_queries: bfloat16 [2, 32768, 1024], P('dp', 'seq')
- grad_keys: bfloat16 [2, 32768, 1024], P('dp', 'seq')
- grad_values: bfloat16 [2, 32768, 1024], P('dp', 'seq')
- weight_grad: float32 [1024, 2048], replicated
Inputs may be any that keep to these rules, and one draw needn't show every extreme that they name: offsets[h] is the residue mod 16 of head h's dilated positions.
All inputs are finite; a program needn't handle non-finite values.
Results may differ from a plain program's by a relative error of at most 0.017.
Values may be sent and summed in bfloat16 or wider, within the bound.
A program may use at most 192 MiB of HBM per device.

v0:
```python
import math

import jax
import jax.numpy as jnp
from jax import lax
from jax.experimental import pallas as pl
from jax.experimental.pallas import tpu as pltpu
from jax.sharding import PartitionSpec as P
MESH = pl.DeviceIdType.MESH

RATE = 16
HEADS = 8
DIM = 128
TOK = 512
PICK = 32
HOLD = 8
SCALE = DIM ** -0.5
LOG2E = math.log2(math.e)
SCALE2 = SCALE * LOG2E
NT = (((1,), (1,)), ((), ()))
TN = (((0,), (0,)), ((), ()))


def mm(a, b, dims=(((1,), (0,)), ((), ()))):
    return lax.dot_general(a, b, dims, preferred_element_type=jnp.float32)


def head_cols(h):
    return pl.ds(pl.multiple_of(h * DIM, DIM), DIM)


def picker(off):
    row = lax.broadcasted_iota(jnp.int32, (PICK, TOK), 0)
    pos = lax.broadcasted_iota(jnp.int32, (PICK, TOK), 1)
    return pos == row * RATE + off


def with_ones(value):
    return jnp.concatenate([value, jnp.ones_like(value)], axis=1)


def softmax_out(q, k, v1):
    s = mm(q, k, NT)
    top = jnp.max(s, axis=1, keepdims=True) * SCALE2
    e = jnp.exp2(s * SCALE2 - top).astype(jnp.bfloat16)
    ov = mm(e, v1)
    total = ov[:, DIM:]
    return ov[:, :DIM] / total, top + jnp.log(total) * LOG2E


def wait_bytes(ref, sem):
    pltpu.make_async_copy(ref, ref, sem).wait()


def far_kernel(off_ref, q_ref, k_ref, v_ref, w_hbm, grad_hbm,
               att_ref, g_ref, lse_ref, delta_ref, dkv_ref, dq_ref,
               w_ref, grad_ref, kv_sel, q_sel, g_sel, os_sel, kv_all, q_all, g_all, os_all,
               back_att, back_stat, got_att, got_stat, near_out, lse_cols, dq_acc,
               load_sem, send_sem, recv_sem):
    dp = lax.axis_index("dp")
    seq = lax.axis_index("seq")
    my_head, my_part = seq // HOLD, seq % HOLD
    load_w = pltpu.make_async_copy(w_hbm, w_ref, load_sem.at[0])
    load_g = pltpu.make_async_copy(grad_hbm, grad_ref, load_sem.at[1])
    load_w.start()
    load_g.start()
    barrier = pltpu.get_barrier_semaphore()

    @pl.loop(1, 64)
    def _(i):
        pl.semaphore_signal(barrier, inc=1, device_id=(dp, lax.rem(seq + i, 64)), device_id_type=MESH)

    @pl.loop(0, HEADS)
    def _(h):
        s = picker(off_ref[h]).astype(jnp.bfloat16)
        kv_sel[h, 0] = mm(s, k_ref[:, head_cols(h)]).astype(jnp.bfloat16)
        kv_sel[h, 1] = mm(s, v_ref[:, head_cols(h)]).astype(jnp.bfloat16)
        q_sel[h] = mm(s, q_ref[:, head_cols(h)]).astype(jnp.bfloat16)

    pl.semaphore_wait(barrier, 63)

    @pl.loop(1, 64)
    def _(i):
        d = lax.rem(seq + i, 64)
        pltpu.make_async_remote_copy(
            src_ref=kv_sel.at[d // HOLD], dst_ref=kv_all.at[:, seq], send_sem=send_sem.at[0], recv_sem=recv_sem.at[0],
            device_id=(dp, d), device_id_type=MESH).start()

    kv_all[:, seq] = kv_sel[my_head]

    def to_group(src, dst, k):
        @pl.loop(1, HEADS)
        def _(i):
            h = lax.rem(my_head + i, HEADS)
            pltpu.make_async_remote_copy(
                src_ref=src.at[h], dst_ref=dst.at[my_head], send_sem=send_sem.at[k], recv_sem=recv_sem.at[k],
                device_id=(dp, h * HOLD + my_part), device_id_type=MESH).start()
        dst[my_head] = src[my_head]

    to_group(q_sel, q_all, 1)

    @pl.loop(0, HEADS)
    def _(h):
        o, lse = softmax_out(q_sel[h], k_ref[:, head_cols(h)], with_ones(v_ref[:, head_cols(h)]))
        os_sel[h, 0] = o
        os_sel[h, 1] = lse

    to_group(os_sel, os_all, 2)
    load_w.wait()
    load_g.wait()

    @pl.loop(0, 4)
    def _(c):
        cols = pl.ds(pl.multiple_of(c * 256, 256), 256)
        g_ref[:, cols] = mm(grad_ref[...], w_ref[cols, :], NT).astype(jnp.bfloat16)

    @pl.loop(0, HEADS)
    def _(h):
        s = picker(off_ref[h]).astype(jnp.bfloat16)
        g_sel[h] = mm(s, g_ref[:, head_cols(h)]).astype(jnp.bfloat16)

    to_group(g_sel, g_all, 3)
    lse_cols[...] = jnp.zeros_like(lse_cols)

    @pl.loop(0, HEADS)
    def _(h):
        v1 = with_ones(v_ref[:, head_cols(h)])
        k = k_ref[:, head_cols(h)]
        for r in range(2):
            rows = slice(r * 256, r * 256 + 256)
            o, lse = softmax_out(q_ref[rows, head_cols(h)], k, v1)
            near_out[rows, head_cols(h)] = o.astype(jnp.bfloat16)
            lane = lax.broadcasted_iota(jnp.int32, (256, 128), 1)
            lse_cols[rows] = jnp.where(lane == h, lse, lse_cols[rows])

    wait_bytes(q_all.at[pl.ds(0, 7)], recv_sem.at[1])
    wait_bytes(kv_all.at[:, pl.ds(0, 63)], recv_sem.at[0])
    q = q_all[...].reshape(256, DIM)
    k = kv_all[0].reshape(2048, DIM)
    v1 = with_ones(kv_all[1].reshape(2048, DIM))
    far = [softmax_out(q[r * 128:r * 128 + 128], k, v1) for r in range(2)]
    far_out = jnp.concatenate([f[0] for f in far], axis=0)
    far_lse = jnp.concatenate([f[1] for f in far], axis=0)
    wait_bytes(os_all.at[pl.ds(0, 7)], recv_sem.at[2])
    near_sel = os_all[:, 0].reshape(256, DIM)
    near_lse = os_all[:, 1].reshape(256, DIM)
    top = jnp.maximum(near_lse, far_lse)
    mixed = top + jnp.log(jnp.exp2(near_lse - top) + jnp.exp2(far_lse - top)) * LOG2E
    att = (jnp.exp2(near_lse - mixed) * near_sel + jnp.exp2(far_lse - mixed) * far_out).astype(jnp.bfloat16)
    back_att[...] = att.reshape(HOLD, PICK, DIM)
    wait_bytes(g_all.at[pl.ds(0, 7)], recv_sem.at[3])
    g = g_all[...].reshape(256, DIM)
    delta = jnp.sum(g.astype(jnp.float32) * att.astype(jnp.float32), axis=1, keepdims=True)
    lane = lax.broadcasted_iota(jnp.int32, (256, DIM), 1)
    stat = jnp.where(lane < 64, mixed, delta)
    back_stat[...] = stat.reshape(HOLD, PICK, DIM)
    to_group(back_att, got_att, 4)
    to_group(back_stat, got_stat, 5)
    stat_t = stat.T
    mixed_lane = stat_t[0:1, :]
    delta_lane = stat_t[64:65, :]
    dq_acc[...] = jnp.zeros_like(dq_acc)

    @pl.loop(0, 4)
    def _(c):
        blocks = pl.ds(c * 16, 16)
        kc = kv_all[0, blocks].reshape(512, DIM)
        vc = kv_all[1, blocks].reshape(512, DIM)
        qq = q_all[...].reshape(256, DIM)
        gg = g_all[...].reshape(256, DIM)
        p = jnp.exp2(mm(kc, qq, NT) * SCALE2 - mixed_lane)
        ds = (p * (mm(vc, gg, NT) - delta_lane)).astype(jnp.bfloat16)
        dkv_ref[0, blocks] = (mm(ds, qq) * SCALE).astype(jnp.bfloat16).reshape(16, PICK, DIM)
        dkv_ref[1, blocks] = mm(p.astype(jnp.bfloat16), gg).astype(jnp.bfloat16).reshape(16, PICK, DIM)
        dq_acc[...] += mm(ds, kc, TN)

    dq_ref[...] = (dq_acc[...] * SCALE).astype(jnp.bfloat16).reshape(HOLD, PICK, DIM)

    lse_t = lse_cols[...].T
    lse_ref[...] = lse_t[0:HEADS, :]
    wait_bytes(got_att.at[pl.ds(0, 7)], recv_sem.at[4])
    wait_bytes(got_stat.at[pl.ds(0, 7)], recv_sem.at[5])

    for h in range(HEADS):
        pick = picker(off_ref[h])
        st = got_stat[h]
        mixed_h = jnp.sum(jnp.where(pick, st[:, 0:1], 0.0), axis=0, keepdims=True)
        delta_h = jnp.sum(jnp.where(pick, st[:, 64:65], 0.0), axis=0, keepdims=True)
        lane1 = lax.rem(lax.broadcasted_iota(jnp.int32, (1, TOK), 1), RATE)
        lse_ref[h:h + 1, :] = jnp.where(lane1 == off_ref[h], mixed_h, lse_ref[h:h + 1, :])
        delta_ref[h:h + 1, :] = delta_h
        cols = slice(h * DIM, h * DIM + DIM)
        put = mm(pick.astype(jnp.bfloat16), got_att[h], TN)
        rowmod = lax.rem(lax.broadcasted_iota(jnp.int32, (TOK, DIM), 0), RATE)
        att_ref[:, cols] = jnp.where(rowmod == off_ref[h], put, near_out[:, cols].astype(jnp.float32)).astype(jnp.bfloat16)

    wait_bytes(kv_all.at[:, pl.ds(0, 63)], send_sem.at[0])
    wait_bytes(q_all.at[pl.ds(0, 7)], send_sem.at[1])
    wait_bytes(os_all.at[pl.ds(0, 7)], send_sem.at[2])
    wait_bytes(g_all.at[pl.ds(0, 7)], send_sem.at[3])
    wait_bytes(got_att.at[pl.ds(0, 7)], send_sem.at[4])
    wait_bytes(got_stat.at[pl.ds(0, 7)], send_sem.at[5])


def far_call(offsets, q, k, v, w, grad):
    bf, f32 = jnp.bfloat16, jnp.float32
    vm = pl.BlockSpec(memory_space=pltpu.VMEM)
    S = jax.ShapeDtypeStruct
    return pl.pallas_call(
        far_kernel,
        out_shape=(S((TOK, 1024), bf), S((TOK, 1024), bf), S((HEADS, TOK), f32), S((HEADS, TOK), f32),
                   S((2, 64, PICK, DIM), bf), S((HOLD, PICK, DIM), bf)),
        in_specs=[pl.BlockSpec(memory_space=pltpu.SMEM), vm, vm, vm, pl.BlockSpec(memory_space=pl.ANY), pl.BlockSpec(memory_space=pl.ANY)],
        out_specs=(vm,) * 6,
        scratch_shapes=[
            pltpu.VMEM((1024, 2048), bf), pltpu.VMEM((TOK, 2048), bf),
            pltpu.VMEM((HEADS, 2, PICK, DIM), bf), pltpu.VMEM((HEADS, PICK, DIM), bf), pltpu.VMEM((HEADS, PICK, DIM), bf),
            pltpu.VMEM((HEADS, 2, PICK, DIM), f32),
            pltpu.VMEM((2, 64, PICK, DIM), bf), pltpu.VMEM((HOLD, PICK, DIM), bf), pltpu.VMEM((HOLD, PICK, DIM), bf),
            pltpu.VMEM((HOLD, 2, PICK, DIM), f32),
            pltpu.VMEM((HOLD, PICK, DIM), bf), pltpu.VMEM((HOLD, PICK, DIM), f32),
            pltpu.VMEM((HOLD, PICK, DIM), bf), pltpu.VMEM((HOLD, PICK, DIM), f32),
            pltpu.VMEM((TOK, 1024), bf), pltpu.VMEM((TOK, 128), f32), pltpu.VMEM((256, DIM), f32),
            pltpu.SemaphoreType.DMA((2,)), pltpu.SemaphoreType.DMA((6,)), pltpu.SemaphoreType.DMA((6,)),
        ],
        compiler_params=pltpu.CompilerParams(collective_id=1, has_side_effects=True, vmem_limit_bytes=60 * 1024 * 1024),
    )(offsets, q, k, v, w, grad)


STRIDES = (16, 4, 1)
ORDERS = ((0, 1, 2), (1, 2, 0), (2, 0, 1))
WIDTHS = (384, 384, 384, 384, 256, 256)
STARTS = (0, 384, 768, 1152, 1536, 1792)
PARTS = [(ORDERS[p % 3], p // 3) for p in range(6)]
STEP_ROWS = (256, 128, 64, 32)
STEP_OFF = (0, 256, 384, 448)


def sum_kernel(off_ref, att_ref, grad_ref, lse_ref, delta_ref, q_hbm, k_hbm, v_hbm, g_hbm, w_hbm, dkv_hbm, dqf_hbm,
               res_hbm, dq_hbm, dk_hbm, dv_hbm, out_ref,
               q_ref, k_ref, v_ref, g_ref, w_ref, res_ref, dq_ref, dk_ref, dv_ref, got_dkv, got_dq,
               flat_t, acc, s0, r0, sbuf, rbuf, last, load_sem, store_sem, far_sem, send_sem, recv_sem):
    dp = lax.axis_index("dp")
    seq = lax.axis_index("seq")
    my_head, my_part = seq // HOLD, seq % HOLD
    coord = [(seq // st) % 4 for st in STRIDES]
    barrier = pltpu.get_barrier_semaphore()
    sibling = (1 - dp, seq)
    pl.semaphore_signal(barrier, inc=1, device_id=sibling, device_id_type=MESH)

    @pl.loop(1, 64)
    def _(i):
        pl.semaphore_signal(barrier, inc=1, device_id=(dp, lax.rem(seq + i, 64)), device_id_type=MESH)

    loads = [pltpu.make_async_copy(s, d, load_sem.at[i]) for i, (s, d) in enumerate(
        ((q_hbm, q_ref), (k_hbm, k_ref), (v_hbm, v_ref), (g_hbm, g_ref), (w_hbm, w_ref)))]
    for load in loads:
        load.start()

    def peer(axis, c):
        return (dp, seq + (c - coord[axis]) * STRIDES[axis])

    flat_t[...] = att_ref[...].T
    mine = pl.multiple_of(dp * 512, 512)
    other = pl.multiple_of((1 - dp) * 512, 512)

    def copy(p, k, src, dst, target):
        return pltpu.make_async_remote_copy(src_ref=src, dst_ref=dst, send_sem=send_sem.at[p, k], recv_sem=recv_sem.at[p, k], device_id=target, device_id_type=MESH)

    cols = [slice(STARTS[p], STARTS[p] + WIDTHS[p]) for p in range(6)]
    started = []
    stores = []
    first = []
    for p in range(6):
        s0[:, cols[p]] = mm(flat_t[pl.ds(other, 512), :], grad_ref[:, cols[p]]).astype(jnp.bfloat16)
        if p == 0:
            pl.semaphore_wait(barrier, 64)
        c = copy(p, 0, s0.at[:, cols[p]], r0.at[:, cols[p]], sibling)
        c.start()
        first.append(c)
    started += first

    own = [pltpu.make_async_copy(dkv_hbm.at[:, seq], got_dkv.at[seq], load_sem.at[5]),
           pltpu.make_async_copy(dqf_hbm.at[my_head], got_dq.at[my_head], load_sem.at[6])]
    for c in own:
        c.start()

    @pl.loop(1, 64)
    def _(i):
        d = lax.rem(seq + i, 64)
        pltpu.make_async_remote_copy(
            src_ref=dkv_hbm.at[:, d], dst_ref=got_dkv.at[seq], send_sem=far_sem.at[0], recv_sem=far_sem.at[1],
            device_id=(dp, d), device_id_type=MESH).start()

    @pl.loop(1, HEADS)
    def _(i):
        h = lax.rem(my_head + i, HEADS)
        pltpu.make_async_remote_copy(
            src_ref=dqf_hbm.at[h], dst_ref=got_dq.at[my_head], send_sem=far_sem.at[2], recv_sem=far_sem.at[3],
            device_id=(dp, h * HOLD + my_part), device_id_type=MESH).start()

    for p in range(6):
        acc[:, cols[p]] = mm(flat_t[pl.ds(mine, 512), :], grad_ref[:, cols[p]])

    def project(c):
        if c == 0:
            loads[4].wait()
        cs = slice(c * 512, c * 512 + 512)
        res_ref[:, cs] = mm(att_ref[...], w_ref[:, cs]).astype(jnp.bfloat16)
        st = pltpu.make_async_copy(res_ref.at[:, cs], res_hbm.at[:, cs], store_sem.at[0, c])
        st.start()
        stores.append(st)

    def returned():
        for load in loads[:4] + own:
            load.wait()
        wait_bytes(got_dkv.at[pl.ds(0, 63)], far_sem.at[1])
        wait_bytes(got_dq.at[pl.ds(0, 7)], far_sem.at[3])

    def near_back(h):
        hs = slice(h * DIM, h * DIM + DIM)
        off = off_ref[h]
        q, k, g = q_ref[:, hs], k_ref[:, hs], g_ref[:, hs]
        probs = jnp.exp2(mm(k, q, NT) * SCALE2 - lse_ref[h:h + 1, :])
        low = probs.astype(jnp.bfloat16)
        prod = probs * mm(v_ref[:, hs], g, NT)
        lane = lax.rem(lax.broadcasted_iota(jnp.int32, (1, TOK), 1), RATE)
        delta = jnp.where(lane == off, delta_ref[h:h + 1, :], jnp.sum(prod, axis=0, keepdims=True))
        ds = (prod - probs * delta).astype(jnp.bfloat16)
        put = (lax.broadcasted_iota(jnp.int32, (TOK, HOLD * PICK), 0)
               == lax.rem(lax.broadcasted_iota(jnp.int32, (TOK, HOLD * PICK), 1), PICK) * RATE + off).astype(jnp.bfloat16)
        far = slice(h * HOLD, h * HOLD + HOLD)
        dv_ref[:, hs] = (mm(low, g) + mm(put, got_dkv[far, 1].reshape(HOLD * PICK, DIM))).astype(jnp.bfloat16)
        dk_ref[:, hs] = (mm(ds, q) * SCALE + mm(put, got_dkv[far, 0].reshape(HOLD * PICK, DIM))).astype(jnp.bfloat16)
        dq_ref[:, hs] = (mm(ds, k, TN) * SCALE + mm(put[:, :PICK], got_dq[h])).astype(jnp.bfloat16)
        for i, (a, b) in enumerate(((dq_ref, dq_hbm), (dk_ref, dk_hbm), (dv_ref, dv_hbm))):
            st = pltpu.make_async_copy(a.at[:, hs], b.at[:, hs], store_sem.at[1 + i, h])
            st.start()
            stores.append(st)

    base = [0] * 6
    flight = [None] * 6
    history = [[] for _ in range(6)]

    def launch(p, s):
        order, swap = PARTS[p]
        axis = order[s // 2]
        c = coord[axis]
        if (s % 2) == swap:
            bit, target = ((c + 1) // 2) % 2, peer(axis, c + 1 - 2 * (c % 2))
        else:
            bit, target = c // 2, peer(axis, 3 - c)
        n = STEP_ROWS[s]
        keep = pl.multiple_of(base[p] + bit * n, n)
        send = pl.multiple_of(base[p] + (1 - bit) * n, n)
        rows = slice(STEP_OFF[s], STEP_OFF[s] + n)
        sbuf[rows, cols[p]] = acc[pl.ds(send, n), cols[p]].astype(jnp.bfloat16)
        cp = copy(p, 1 + s, sbuf.at[rows, cols[p]], rbuf.at[rows, cols[p]], target)
        cp.start()
        started.append(cp)
        history[p].append((keep, send, target))
        base[p] = keep
        flight[p] = cp

    for p in range(6):
        first[p].wait_recv()
        acc[:, cols[p]] += r0[:, cols[p]].astype(jnp.float32)
        launch(p, 0)
    for c in range(4):
        project(c)
    lasts = [None] * 6
    for s in range(4):
        n = STEP_ROWS[s]
        rows = slice(STEP_OFF[s], STEP_OFF[s] + n)
        for p in range(6):
            flight[p].wait_recv()
            acc[pl.ds(base[p], n), cols[p]] += rbuf[rows, cols[p]].astype(jnp.float32)
            if s < 3:
                launch(p, s + 1)
            else:
                axis = PARTS[p][0][2]
                sbuf[480:512, cols[p]] = acc[pl.ds(base[p], 32), cols[p]].astype(jnp.bfloat16)
                lasts[p] = []
                for d in (1, 2, 3):
                    cp = copy(p, 4 + d, sbuf.at[480:512, cols[p]], last.at[d - 1, :, cols[p]], peer(axis, (coord[axis] + d) % 4))
                    cp.start()
                    started.append(cp)
                    lasts[p].append(cp)
        if s == 0:
            returned()
        near_back(s)
    gather = [None] * 6
    for p in range(6):
        for d in (1, 2, 3):
            lasts[p][d - 1].wait_recv()
        total = sbuf[480:512, cols[p]].astype(jnp.float32)
        for d in (1, 2, 3):
            total = total + last[d - 1, :, cols[p]].astype(jnp.float32)
        rows = pl.ds(pl.multiple_of(mine + base[p], 32), 32)
        out_ref[rows, cols[p]] = total.astype(jnp.bfloat16)
        here = out_ref.at[rows, cols[p]]
        cp = copy(p, 8, here, here, history[p][3][2])
        cp.start()
        started.append(cp)
        gather[p] = cp
    near_back(4)
    final = []
    for s in (3, 2, 1, 0):
        for p in range(6):
            gather[p].wait_recv()
            n = STEP_ROWS[s]
            if s > 0:
                start = pl.multiple_of(mine + history[p][s - 1][0], 2 * n)
                here = out_ref.at[pl.ds(start, 2 * n), cols[p]]
                cp = copy(p, 12 - s, here, here, history[p][s - 1][2])
                cp.start()
                started.append(cp)
                gather[p] = cp
                if s == 1:
                    final.append(copy(p, 12, here, here, sibling))
                    final[-1].start()
            else:
                start = pl.multiple_of(mine + history[p][0][1], n)
                here = out_ref.at[pl.ds(start, n), cols[p]]
                final.append(copy(p, 13, here, here, sibling))
                final[-1].start()
        if s > 0:
            near_back(8 - s)
    for cp in final:
        cp.wait_recv()
    for cp in started + final:
        cp.wait_send()
    for st in stores:
        st.wait()
    wait_bytes(got_dkv.at[pl.ds(0, 63)], far_sem.at[0])
    wait_bytes(got_dq.at[pl.ds(0, 7)], far_sem.at[2])


def sum_call(offsets, att, grad, lse, delta, q, k, v, g, w, dkv, dqf):
    bf, f32 = jnp.bfloat16, jnp.float32
    vm = pl.BlockSpec(memory_space=pltpu.VMEM)
    anyspace = pl.BlockSpec(memory_space=pl.ANY)
    S = jax.ShapeDtypeStruct
    V = pltpu.VMEM
    return pl.pallas_call(
        sum_kernel,
        out_shape=(S((TOK, 2048), bf), S((TOK, 1024), bf), S((TOK, 1024), bf), S((TOK, 1024), bf), S((1024, 2048), bf)),
        in_specs=[pl.BlockSpec(memory_space=pltpu.SMEM)] + [vm] * 4 + [anyspace] * 7,
        out_specs=(anyspace,) * 4 + (vm,),
        scratch_shapes=[
            V((TOK, 1024), bf), V((TOK, 1024), bf), V((TOK, 1024), bf), V((TOK, 1024), bf), V((1024, 2048), bf),
            V((TOK, 2048), bf), V((TOK, 1024), bf), V((TOK, 1024), bf), V((TOK, 1024), bf),
            V((64, 2, PICK, DIM), bf), V((HEADS, PICK, DIM), bf),
            V((1024, 512), bf), V((512, 2048), f32), V((512, 2048), bf), V((512, 2048), bf), V((512, 2048), bf),
            V((512, 2048), bf), V((3, 32, 2048), bf),
            pltpu.SemaphoreType.DMA((7,)), pltpu.SemaphoreType.DMA((4, 8)), pltpu.SemaphoreType.DMA((4,)),
            pltpu.SemaphoreType.DMA((6, 14)), pltpu.SemaphoreType.DMA((6, 14)),
        ],
        compiler_params=pltpu.CompilerParams(collective_id=0, has_side_effects=True, vmem_limit_bytes=60 * 1024 * 1024),
    )(offsets, att, grad, lse, delta, q, k, v, g, w, dkv, dqf)


def per_device(queries, keys, values, offsets, out_weight, grad_out):
    q, k, v, grad = queries[0], keys[0], values[0], grad_out[0]
    att, g, lse, delta, dkv, dqf = far_call(offsets, q, k, v, out_weight, grad)
    res, dq, dk, dv, total = sum_call(offsets, att, grad, lse, delta, q, k, v, g, out_weight, dkv, dqf)
    weight_grad = total.astype(jnp.float32) * (1.0 / math.sqrt(65536))
    return res[None], dq[None], dk[None], dv[None], weight_grad


def solution(mesh):
    split = P("dp", "seq", None)
    return jax.shard_map(
        per_device, mesh=mesh, in_specs=(split, split, split, P(), P(), split),
        out_specs=(split, split, split, split, P()), check_vma=False)
```

profile of v0, /device:TPU:1, one launch (start us, length us, event | category | flops | bytes accessed | tf_op | source)
XLA Modules:
  0.0 117.4 jit_solution(3961047187437969626)
XLA Ops:
  0.6 38.5 %shard_map.101 = (bf16[512,1024]{1,0:T(8,128)(2,1)}, bf16[512,1024]{1,0:T(8,128)(2,1)}, f32[8,512]{1,0:T(8,128)}, f32[8,512]{1,0:T(8,128)}, bf16[2,64,32,128]{3,...) custom-call(s32[8]{0:T(128)} %off_ref.3, bf16[512,1024]{1,0:T(8,128)(2,1)} %bitcast.10, bf16[512,1024]{1,0:T(8,128)(2,1)} %bitcast.12, ...), custom_call_target="tpu_custom_call" | custom-call | tf_op jit(solution)/shard_map/pallas_call | solution.py:209
  39.1 66.5 %shard_map.102 = (bf16[512,2048]{1,0:T(8,128)(2,1)}, bf16[512,1024]{1,0:T(8,128)(2,1)}, bf16[512,1024]{1,0:T(8,128)(2,1)}, bf16[512,1024]{1,0:T(8,128)(2,1)}, bf16[1024,2048]{1,0:T(8,128)(2,1)}) custom-call(s32[8]{0:T(128)} %off_ref.3, bf16[512,1024]{1,0:T(8,128)(2,1)} %get-tuple-element.16.att_ref, bf16[512,2048]{1,0:T(8,128)(2,1)} %bitcast.9, ...), custom_call_target="tpu_custom_call" | custom-call | tf_op jit(solution)/shard_map/pallas_call | solution.py:445
  105.6 0.0 copy-start
  105.6 6.9 %convert_multiply_fusion = f32[1024,2048]{1,0:T(8,128)} fusion(bf16[1024,2048]{1,0:T(8,128)(2,1)} %get-tuple-element.26), kind=kLoop, calls=%fused_computation | loop fusion | flops 4194304 | bytes 12582912 | tf_op jit(solution)/shard_map/mul | solution.py:467
  112.5 0.0 copy-done
  112.5 0.0 copy-start.3
  112.5 0.0 copy-start.2
  112.5 0.0 copy-start.1
  112.6 1.3 %copy.15 = bf16[1,512,2048]{2,1,0:T(8,128)(2,1)} copy(bf16[1,512,2048]{2,1,0:T(8,128)(2,1)S(1)} %bitcast.16) | data formatting | bytes 4194304
  113.9 0.6 copy-done.3
  114.5 1.0 copy.16
  115.4 0.0 copy-done.2
  115.5 1.0 copy.17
  116.4 0.0 copy-done.1
  116.4 1.0 copy.18
Async XLA Ops:
  105.6 6.9 %copy-start = (bf16[512,2048]{1,0:T(8,128)(2,1)S(1)}, bf16[512,2048]{1,0:T(8,128)(2,1)}, u32[]{:S(2)}) copy-start(bf16[512,2048]{1,0:T(8,128)(2,1)} %get-tuple-element.22) | copy-start | bytes 6291460
  112.5 1.9 %copy-start.3 = (bf16[512,1024]{1,0:T(8,128)(2,1)S(1)}, bf16[512,1024]{1,0:T(8,128)(2,1)}, u32[]{:S(2)}) copy-start(bf16[512,1024]{1,0:T(8,128)(2,1)} %get-tuple-element.23) | copy-start | bytes 3145732
  112.5 2.9 %copy-start.2 = (bf16[512,1024]{1,0:T(8,128)(2,1)S(1)}, bf16[512,1024]{1,0:T(8,128)(2,1)}, u32[]{:S(2)}) copy-start(bf16[512,1024]{1,0:T(8,128)(2,1)} %get-tuple-element.24) | copy-start | bytes 3145732
  112.5 3.9 %copy-start.1 = (bf16[512,1024]{1,0:T(8,128)(2,1)S(1)}, bf16[512,1024]{1,0:T(8,128)(2,1)}, u32[]{:S(2)}) copy-start(bf16[512,1024]{1,0:T(8,128)(2,1)} %get-tuple-element.25) | copy-start | bytes 3145732
where the time goes:
time: 118 us; the launch traced here: 117 us
  Pallas kernels  105 us (89%)
  other arithmetic  6.93 us (6%)
  local copies, waits for them, and re-layouts  4.85 us (4%)
    pallas_call x1, Pallas kernels, sum_call(): pl.pallas_call(sum_kernel, out_shape=(S((TOK, 2048), bf), S((TOK, 1024),...  66.5 us
    pallas_call x1, Pallas kernels, far_call(): pl.pallas_call(far_kernel, out_shape=(S((TOK, 1024), bf), S((TOK, 1024),...  38.5 us
    mul x1, other arithmetic, per_device(): weight_grad = total.astype(jnp.float32) * (1.0 / math.sqrt(65536))  6.93 us
    unnamed x12, local copies, waits for them, and re-layouts  4.85 us

commit v1 on v0

v1 whole, which is shorter than its diff:
```python
import math

import jax
import jax.numpy as jnp
from jax import lax
from jax.experimental import pallas as pl
from jax.experimental.pallas import tpu as pltpu
from jax.sharding import PartitionSpec as P

MESH = pl.DeviceIdType.MESH

RATE = 16
HEADS = 8
DIM = 128
TOK = 512
PICK = 32
HOLD = 8
SCALE = DIM ** -0.5
LOG2E = math.log2(math.e)
SCALE2 = SCALE * LOG2E
NT = (((1,), (1,)), ((), ()))
TN = (((0,), (0,)), ((), ()))


def mm(a, b, dims=(((1,), (0,)), ((), ()))):
    return lax.dot_general(a, b, dims, preferred_element_type=jnp.float32)


def head_cols(h):
    return pl.ds(pl.multiple_of(h * DIM, DIM), DIM)


def picker(off):
    row = lax.broadcasted_iota(jnp.int32, (PICK, TOK), 0)
    pos = lax.broadcasted_iota(jnp.int32, (PICK, TOK), 1)
    return pos == row * RATE + off


def with_ones(value):
    return jnp.concatenate([value, jnp.ones_like(value)], axis=1)


def softmax_out(q, k, v1):
    s = mm(q, k, NT)
    top = jnp.max(s, axis=1, keepdims=True) * SCALE2
    e = jnp.exp2(s * SCALE2 - top).astype(jnp.bfloat16)
    ov = mm(e, v1)
    total = ov[:, DIM:]
    return ov[:, :DIM] / total, top + jnp.log(total) * LOG2E


def wait_bytes(ref, sem):
    pltpu.make_async_copy(ref, ref, sem).wait()


STRIDES = (16, 4, 1)
WIDTHS = (384, 384, 384, 384, 256, 256)
STARTS = (0, 384, 768, 1152, 1536, 1792)
COLS = [slice(a, a + b) for a, b in zip(STARTS, WIDTHS)]
ORDERS = ((0, 1, 2), (1, 2, 0), (2, 0, 1)) * 2


def layer_kernel(off_ref, q_hbm, k_hbm, v_hbm, w_hbm, grad_hbm,
                 res_hbm, dq_hbm, dk_hbm, dv_hbm, total_hbm,
                 q_ref, k_ref, v_ref, w_ref, grad_ref, g_ref, att_ref, res_ref, dq_ref, dk_ref, dv_ref,
                 kv_sel, q_sel, g_sel, os_sel, kv_all, q_all, g_all, os_all,
                 back_att, back_stat, got_att, got_stat, dkv, dqf, got_dkv, got_dq,
                 near_t, lse_cols, lse_ref, delta_ref, dq_acc, dqn_acc, dk_acc, dv_acc,
                 acc, s0, r0, sbuf, rbuf1, rbuf2, last, total_ref,
                 load_sem, store_sem, far_send, far_recv, send_sem, recv_sem):
    dp = lax.axis_index("dp")
    seq = lax.axis_index("seq")
    my_head, my_part = seq // HOLD, seq % HOLD
    coord = [(seq // st) % 4 for st in STRIDES]
    sibling = (1 - dp, seq)
    barrier = pltpu.get_barrier_semaphore()
    loads = [pltpu.make_async_copy(s, d, load_sem.at[i]) for i, (s, d) in enumerate(
        ((k_hbm, k_ref), (v_hbm, v_ref), (q_hbm, q_ref), (w_hbm, w_ref), (grad_hbm, grad_ref)))]
    for load in loads:
        load.start()
    pl.semaphore_signal(barrier, inc=1, device_id=sibling, device_id_type=MESH)

    @pl.loop(1, 64)
    def _(i):
        pl.semaphore_signal(barrier, inc=1, device_id=(dp, lax.rem(seq + i, 64)), device_id_type=MESH)

    started = []
    stores = []

    def store(src, dst, sem):
        st = pltpu.make_async_copy(src, dst, sem)
        st.start()
        stores.append(st)

    def to_group(src, dst, k):
        @pl.loop(1, HEADS)
        def _(i):
            h = lax.rem(my_head + i, HEADS)
            pltpu.make_async_remote_copy(
                src_ref=src.at[h], dst_ref=dst.at[my_head], send_sem=far_send.at[k], recv_sem=far_recv.at[k],
                device_id=(dp, h * HOLD + my_part), device_id_type=MESH).start()
        dst[my_head] = src[my_head]

    loads[0].wait()
    loads[1].wait()

    @pl.loop(0, HEADS)
    def _(h):
        s = picker(off_ref[h]).astype(jnp.bfloat16)
        kv_sel[h, 0] = mm(s, k_ref[:, head_cols(h)]).astype(jnp.bfloat16)
        kv_sel[h, 1] = mm(s, v_ref[:, head_cols(h)]).astype(jnp.bfloat16)

    pl.semaphore_wait(barrier, 64)

    @pl.loop(1, 64)
    def _(i):
        d = lax.rem(seq + i, 64)
        pltpu.make_async_remote_copy(
            src_ref=kv_sel.at[d // HOLD], dst_ref=kv_all.at[:, seq], send_sem=far_send.at[0], recv_sem=far_recv.at[0],
            device_id=(dp, d), device_id_type=MESH).start()

    kv_all[:, seq] = kv_sel[my_head]

    loads[2].wait()

    @pl.loop(0, HEADS)
    def _(h):
        s = picker(off_ref[h]).astype(jnp.bfloat16)
        q_sel[h] = mm(s, q_ref[:, head_cols(h)]).astype(jnp.bfloat16)

    to_group(q_sel, q_all, 1)

    @pl.loop(0, HEADS)
    def _(h):
        o, lse = softmax_out(q_sel[h], k_ref[:, head_cols(h)], with_ones(v_ref[:, head_cols(h)]))
        os_sel[h, 0] = o
        os_sel[h, 1] = lse

    to_group(os_sel, os_all, 2)

    loads[3].wait()
    loads[4].wait()

    @pl.loop(0, 4)
    def _(c):
        cols = pl.ds(pl.multiple_of(c * 256, 256), 256)
        g_ref[:, cols] = mm(grad_ref[...], w_ref[cols, :], NT).astype(jnp.bfloat16)

    @pl.loop(0, HEADS)
    def _(h):
        s = picker(off_ref[h]).astype(jnp.bfloat16)
        g_sel[h] = mm(s, g_ref[:, head_cols(h)]).astype(jnp.bfloat16)

    to_group(g_sel, g_all, 3)

    lse_cols[...] = jnp.zeros_like(lse_cols)

    @pl.loop(0, HEADS)
    def _(h):
        v1 = with_ones(v_ref[:, head_cols(h)])
        k = k_ref[:, head_cols(h)]
        for r in range(2):
            rows = slice(r * 256, r * 256 + 256)
            o, lse = softmax_out(q_ref[rows, head_cols(h)], k, v1)
            near_t[head_cols(h), rows] = o.astype(jnp.bfloat16).T
            lane = lax.broadcasted_iota(jnp.int32, (256, 128), 1)
            lse_cols[rows] = jnp.where(lane == h, lse, lse_cols[rows])

    wait_bytes(q_all.at[pl.ds(0, 7)], far_recv.at[1])
    wait_bytes(kv_all.at[:, pl.ds(0, 63)], far_recv.at[0])
    q = q_all[...].reshape(256, DIM)
    k = kv_all[0].reshape(2048, DIM)
    v1 = with_ones(kv_all[1].reshape(2048, DIM))
    far = [softmax_out(q[r * 128:r * 128 + 128], k, v1) for r in range(2)]
    far_out = jnp.concatenate([f[0] for f in far], axis=0)
    far_lse = jnp.concatenate([f[1] for f in far], axis=0)
    wait_bytes(os_all.at[pl.ds(0, 7)], far_recv.at[2])
    near_sel = os_all[:, 0].reshape(256, DIM)
    near_lse = os_all[:, 1].reshape(256, DIM)
    top = jnp.maximum(near_lse, far_lse)
    mixed = top + jnp.log(jnp.exp2(near_lse - top) + jnp.exp2(far_lse - top)) * LOG2E
    att = (jnp.exp2(near_lse - mixed) * near_sel + jnp.exp2(far_lse - mixed) * far_out).astype(jnp.bfloat16)
    back_att[...] = att.reshape(HOLD, PICK, DIM)
    to_group(back_att, got_att, 4)
    wait_bytes(g_all.at[pl.ds(0, 7)], far_recv.at[3])
    g = g_all[...].reshape(256, DIM)
    delta = jnp.sum(g.astype(jnp.float32) * att.astype(jnp.float32), axis=1, keepdims=True)
    lane = lax.broadcasted_iota(jnp.int32, (256, DIM), 1)
    stat = jnp.where(lane < 64, mixed, delta)
    back_stat[...] = stat.reshape(HOLD, PICK, DIM)
    to_group(back_stat, got_stat, 5)
    stat_t = stat.T
    mixed_lane = stat_t[0:1, :]
    delta_lane = stat_t[64:65, :]
    dq_acc[...] = jnp.zeros_like(dq_acc)

    @pl.loop(0, 4)
    def _(c):
        blocks = pl.ds(c * 16, 16)
        kc = kv_all[0, blocks].reshape(512, DIM)
        vc = kv_all[1, blocks].reshape(512, DIM)
        qq = q_all[...].reshape(256, DIM)
        gg = g_all[...].reshape(256, DIM)
        p = jnp.exp2(mm(kc, qq, NT) * SCALE2 - mixed_lane)
        ds = (p * (mm(vc, gg, NT) - delta_lane)).astype(jnp.bfloat16)
        dkv[0, blocks] = (mm(ds, qq) * SCALE).astype(jnp.bfloat16).reshape(16, PICK, DIM)
        dkv[1, blocks] = mm(p.astype(jnp.bfloat16), gg).astype(jnp.bfloat16).reshape(16, PICK, DIM)
        dq_acc[...] += mm(ds, kc, TN)

    dqf[...] = (dq_acc[...] * SCALE).astype(jnp.bfloat16).reshape(HOLD, PICK, DIM)

    @pl.loop(1, 64)
    def _(i):
        d = lax.rem(seq + i, 64)
        pltpu.make_async_remote_copy(
            src_ref=dkv.at[:, d], dst_ref=got_dkv.at[seq], send_sem=far_send.at[6], recv_sem=far_recv.at[6],
            device_id=(dp, d), device_id_type=MESH).start()

    got_dkv[seq] = dkv[:, seq]
    to_group(dqf, got_dq, 7)

    wait_bytes(got_att.at[pl.ds(0, 7)], far_recv.at[4])
    lane1 = lax.rem(lax.broadcasted_iota(jnp.int32, (1, TOK), 1), RATE)
    for h in range(HEADS):
        rows = slice(h * DIM, h * DIM + DIM)
        put = mm(got_att[h], picker(off_ref[h]).astype(jnp.bfloat16), TN)
        near_t[rows, :] = jnp.where(lane1 == off_ref[h], put, near_t[rows, :].astype(jnp.float32)).astype(jnp.bfloat16)

    def peer(axis, d):
        c = lax.rem(coord[axis] + d, 4)
        return c, (dp, seq + (c - coord[axis]) * STRIDES[axis])

    def copy(p, k, src, dst, target):
        cp = pltpu.make_async_remote_copy(
            src_ref=src, dst_ref=dst, send_sem=send_sem.at[p, k], recv_sem=recv_sem.at[p, k],
            device_id=target, device_id_type=MESH)
        cp.start()
        started.append(cp)
        return cp

    mine = pl.multiple_of(dp * 512, 512)
    other = pl.multiple_of((1 - dp) * 512, 512)
    first = []
    for p in range(6):
        s0[:, COLS[p]] = mm(near_t[pl.ds(other, 512), :], grad_ref[:, COLS[p]]).astype(jnp.bfloat16)
        first.append(copy(p, 0, s0.at[:, COLS[p]], r0.at[:, COLS[p]], sibling))
    for p in range(6):
        acc[:, COLS[p]] = mm(near_t[pl.ds(mine, 512), :], grad_ref[:, COLS[p]])

    flight = [None] * 6

    def send_rows(p, level, base, n, buf, landing):
        axis = ORDERS[p][level]
        flight[p] = []
        for d in (1, 2, 3):
            c, target = peer(axis, d)
            rows = slice((d - 1) * n, d * n)
            buf[rows, COLS[p]] = acc[pl.ds(pl.multiple_of(base + c * n, n), n), COLS[p]].astype(jnp.bfloat16)
            flight[p].append(copy(p, 1 + 3 * level + d - 1, buf.at[rows, COLS[p]], landing.at[rows, COLS[p]], target))

    base1 = []
    for p in range(6):
        first[p].wait_recv()
        acc[:, COLS[p]] += r0[:, COLS[p]].astype(jnp.float32)
        send_rows(p, 0, 0, 128, sbuf, rbuf1)
        base1.append(pl.multiple_of(coord[ORDERS[p][0]] * 128, 128))

    def statistics():
        lse_ref[...] = lse_cols[...].T[0:HEADS, :]
        wait_bytes(got_stat.at[pl.ds(0, 7)], far_recv.at[5])
        for h in range(HEADS):
            pick = picker(off_ref[h])
            st = got_stat[h]
            mixed_h = jnp.sum(jnp.where(pick, st[:, 0:1], 0.0), axis=0, keepdims=True)
            lse_ref[h:h + 1, :] = jnp.where(lane1 == off_ref[h], mixed_h, lse_ref[h:h + 1, :])
            delta_ref[h:h + 1, :] = jnp.sum(jnp.where(pick, st[:, 64:65], 0.0), axis=0, keepdims=True)

    def project(c):
        cs = slice(c * 512, c * 512 + 512)
        res_ref[:, cs] = mm(att_ref[...], w_ref[:, cs]).astype(jnp.bfloat16)
        store(res_ref.at[:, cs], res_hbm.at[:, cs], store_sem.at[0, c])

    def returned():
        wait_bytes(got_dkv.at[pl.ds(0, 63)], far_recv.at[6])
        wait_bytes(got_dq.at[pl.ds(0, 7)], far_recv.at[7])

    def near_back(h):
        hs = slice(h * DIM, h * DIM + DIM)
        off = off_ref[h]
        q, k, g = q_ref[:, hs], k_ref[:, hs], g_ref[:, hs]
        probs = jnp.exp2(mm(k, q, NT) * SCALE2 - lse_ref[h:h + 1, :])
        low = probs.astype(jnp.bfloat16)
        prod = probs * mm(v_ref[:, hs], g, NT)
        delta = jnp.where(lane1 == off, delta_ref[h:h + 1, :], jnp.sum(prod, axis=0, keepdims=True))
        ds = (prod - probs * delta).astype(jnp.bfloat16)
        dv_acc[:, hs] = mm(low, g)
        dk_acc[:, hs] = mm(ds, q) * SCALE
        dqn_acc[:, hs] = mm(ds, k, TN) * SCALE

    def deposit(h):
        hs = slice(h * DIM, h * DIM + DIM)
        off = off_ref[h]
        put = (lax.broadcasted_iota(jnp.int32, (TOK, HOLD * PICK), 0)
               == lax.rem(lax.broadcasted_iota(jnp.int32, (TOK, HOLD * PICK), 1), PICK) * RATE + off).astype(jnp.bfloat16)
        far = slice(h * HOLD, h * HOLD + HOLD)
        dv_ref[:, hs] = (dv_acc[:, hs] + mm(put, got_dkv[far, 1].reshape(HOLD * PICK, DIM))).astype(jnp.bfloat16)
        dk_ref[:, hs] = (dk_acc[:, hs] + mm(put, got_dkv[far, 0].reshape(HOLD * PICK, DIM))).astype(jnp.bfloat16)
        dq_ref[:, hs] = (dqn_acc[:, hs] + mm(put[:, :PICK], got_dq[h])).astype(jnp.bfloat16)
        for i, (a, b) in enumerate(((dq_ref, dq_hbm), (dk_ref, dk_hbm), (dv_ref, dv_hbm))):
            store(a.at[:, hs], b.at[:, hs], store_sem.at[1 + i, h])

    att_ref[...] = near_t[...].T
    for c in range(4):
        project(c)
    statistics()
    near_back(0)
    near_back(1)
    near_back(2)

    def add_received(p, base, n, landing):
        for cp in flight[p]:
            cp.wait_recv()
        rows = pl.ds(pl.multiple_of(base, n), n)
        total = acc[rows, COLS[p]]
        for d in range(3):
            total += landing[d * n:d * n + n, COLS[p]].astype(jnp.float32)
        acc[rows, COLS[p]] = total

    base2 = []
    for p in range(6):
        add_received(p, base1[p], 128, rbuf1)
        send_rows(p, 1, base1[p], 32, sbuf.at[384:480], rbuf2)
        base2.append(pl.multiple_of(base1[p] + coord[ORDERS[p][1]] * 32, 32))
    near_back(3)
    near_back(4)
    for p in range(6):
        add_received(p, base2[p], 32, rbuf2)
        axis = ORDERS[p][2]
        here = coord[axis]
        last[here, :, COLS[p]] = acc[pl.ds(base2[p], 32), COLS[p]].astype(jnp.bfloat16)
        flight[p] = []
        for d in (1, 2, 3):
            _, target = peer(axis, d)
            flight[p].append(copy(p, 6 + d, last.at[here, :, COLS[p]], last.at[here, :, COLS[p]], target))
    near_back(5)
    near_back(6)
    for p in range(6):
        for cp in flight[p]:
            cp.wait_recv()
        total = last[0, :, COLS[p]].astype(jnp.float32)
        for j in (1, 2, 3):
            total += last[j, :, COLS[p]].astype(jnp.float32)
        rows = pl.ds(pl.multiple_of(mine + base2[p], 32), 32)
        total_ref[rows, COLS[p]] = total.astype(jnp.bfloat16)
        block = total_ref.at[rows, COLS[p]]
        flight[p] = [copy(p, 9 + d, block, block, peer(ORDERS[p][1], d)[1]) for d in (1, 2, 3)]
    near_back(7)
    final = []
    for p in range(6):
        for cp in flight[p]:
            cp.wait_recv()
        block = total_ref.at[pl.ds(pl.multiple_of(mine + base1[p], 128), 128), COLS[p]]
        flight[p] = [copy(p, 12 + d, block, block, peer(ORDERS[p][0], d)[1]) for d in (1, 2, 3)]
        final.append(copy(p, 16, block, block, sibling))
    returned()
    for h in range(HEADS):
        deposit(h)
    for p in range(6):
        for d in (1, 2, 3):
            flight[p][d - 1].wait_recv()
            c = lax.rem(coord[ORDERS[p][0]] + 4 - d, 4)
            block = total_ref.at[pl.ds(pl.multiple_of(mine + c * 128, 128), 128), COLS[p]]
            final.append(copy(p, 16 + d, block, block, sibling))
    mine_out = pltpu.make_async_copy(total_ref.at[pl.ds(mine, 512)], total_hbm.at[pl.ds(mine, 512)], load_sem.at[5])
    mine_out.start()
    for cp in final:
        cp.wait_recv()
    other_out = pltpu.make_async_copy(total_ref.at[pl.ds(other, 512)], total_hbm.at[pl.ds(other, 512)], load_sem.at[6])
    other_out.start()
    for cp in started:
        cp.wait_send()
    for st in stores:
        st.wait()
    wait_bytes(kv_all.at[:, pl.ds(0, 63)], far_send.at[0])
    for i, ref in ((1, q_all), (2, os_all), (3, g_all), (4, got_att), (5, got_stat), (7, got_dq)):
        wait_bytes(ref.at[pl.ds(0, 7)], far_send.at[i])
    wait_bytes(got_dkv.at[pl.ds(0, 63)], far_send.at[6])
    mine_out.wait()
    other_out.wait()


def layer_call(offsets, q, k, v, w, grad):
    bf, f32 = jnp.bfloat16, jnp.float32
    hbm = pl.BlockSpec(memory_space=pl.ANY)
    S = jax.ShapeDtypeStruct
    V = pltpu.VMEM
    wide, flat = (TOK, 2048), (TOK, 1024)
    rows = (HEADS, PICK, DIM)
    return pl.pallas_call(
        layer_kernel,
        out_shape=(S(wide, bf), S(flat, bf), S(flat, bf), S(flat, bf), S((1024, 2048), bf)),
        in_specs=[pl.BlockSpec(memory_space=pltpu.SMEM)] + [hbm] * 5,
        out_specs=(hbm,) * 5,
        scratch_shapes=[
            V(flat, bf), V(flat, bf), V(flat, bf), V((1024, 2048), bf), V(wide, bf), V(flat, bf), V(flat, bf),
            V(wide, bf), V(flat, bf), V(flat, bf), V(flat, bf),
            V((HEADS, 2, PICK, DIM), bf), V(rows, bf), V(rows, bf), V((HEADS, 2, PICK, DIM), f32),
            V((2, 64, PICK, DIM), bf), V(rows, bf), V(rows, bf), V((HOLD, 2, PICK, DIM), f32),
            V(rows, bf), V(rows, f32), V(rows, bf), V(rows, f32),
            V((2, 64, PICK, DIM), bf), V(rows, bf), V((64, 2, PICK, DIM), bf), V(rows, bf),
            V((1024, TOK), bf), V((TOK, 128), f32), V((HEADS, TOK), f32), V((HEADS, TOK), f32), V((256, DIM), f32),
            V(flat, f32), V(flat, f32), V(flat, f32),
            V(wide, f32), V(wide, bf), V(wide, bf), V(wide, bf), V((384, 2048), bf), V((96, 2048), bf),
            V((4, 32, 2048), bf), V((1024, 2048), bf),
            pltpu.SemaphoreType.DMA((7,)), pltpu.SemaphoreType.DMA((4, 8)),
            pltpu.SemaphoreType.DMA((8,)), pltpu.SemaphoreType.DMA((8,)),
            pltpu.SemaphoreType.DMA((6, 20)), pltpu.SemaphoreType.DMA((6, 20)),
        ],
        compiler_params=pltpu.CompilerParams(collective_id=0, has_side_effects=True, vmem_limit_bytes=60 * 1024 * 1024),
    )(offsets, q, k, v, w, grad)


def finish_kernel(scale, total_hbm, res_hbm, dq_hbm, dk_hbm, dv_hbm, wg_out, res_out, dq_out, dk_out, dv_out,
                  low, wide, res_ref, dq_ref, dk_ref, dv_ref, copy_sem, in_sem, out_sem):
    pieces = [slice(i * 128, i * 128 + 128) for i in range(8)]
    ins = [pltpu.make_async_copy(total_hbm.at[rows], low.at[rows], in_sem.at[i]) for i, rows in enumerate(pieces)]
    for cp in ins:
        cp.start()
    rest = ((res_hbm, res_ref, res_out), (dq_hbm, dq_ref, dq_out), (dk_hbm, dk_ref, dk_out), (dv_hbm, dv_ref, dv_out))
    copies = [pltpu.make_async_copy(a, b, copy_sem.at[0, i]) for i, (a, b, _) in enumerate(rest)]
    for cp in copies:
        cp.start()
    outs = []
    for i, rows in enumerate(pieces):
        ins[i].wait()
        wide[rows] = low[rows].astype(jnp.float32) * scale
        outs.append(pltpu.make_async_copy(wide.at[rows], wg_out.at[rows], out_sem.at[i]))
        outs[-1].start()
    for i, (_, b, c) in enumerate(rest):
        copies[i].wait()
        outs.append(pltpu.make_async_copy(b, c, copy_sem.at[1, i]))
        outs[-1].start()
    for cp in outs:
        cp.wait()


def finish_call(total, res, dq, dk, dv):
    bf = jnp.bfloat16
    hbm = pl.BlockSpec(memory_space=pl.ANY)
    S = jax.ShapeDtypeStruct
    flat = S((TOK, 1024), bf)

    def kernel(*refs):
        finish_kernel(1.0 / math.sqrt(65536), *refs)

    return pl.pallas_call(
        kernel,
        out_shape=(S((1024, 2048), jnp.float32), S((TOK, 2048), bf), flat, flat, flat),
        in_specs=[hbm] * 5,
        out_specs=(hbm,) * 5,
        scratch_shapes=[pltpu.VMEM((1024, 2048), bf), pltpu.VMEM((1024, 2048), jnp.float32),
                        pltpu.VMEM((TOK, 2048), bf), pltpu.VMEM((TOK, 1024), bf), pltpu.VMEM((TOK, 1024), bf),
                        pltpu.VMEM((TOK, 1024), bf), pltpu.SemaphoreType.DMA((2, 4)), pltpu.SemaphoreType.DMA((8,)), pltpu.SemaphoreType.DMA((8,))],
        compiler_params=pltpu.CompilerParams(vmem_limit_bytes=60 * 1024 * 1024),
    )(total, res, dq, dk, dv)


def per_device(queries, keys, values, offsets, out_weight, grad_out):
    res, dq, dk, dv, total = layer_call(offsets, queries[0], keys[0], values[0], out_weight, grad_out[0])
    weight_grad, res, dq, dk, dv = finish_call(total, res, dq, dk, dv)
    return res[None], dq[None], dk[None], dv[None], weight_grad


def solution(mesh):
    split = P("dp", "seq", None)
    return jax.shard_map(
        per_device, mesh=mesh, in_specs=(split, split, split, P(), P(), split),
        out_specs=(split, split, split, split, P()), check_vma=False)
```

time: 118 us -> 92.5 us (0.78)
  Pallas kernels: 105 us -> 91.6 us
  other arithmetic: 6.93 us -> 0 us
  local copies, waits for them, and re-layouts: 4.85 us -> 0 us
    pallas_call x2, Pallas kernels: 105 us -> 91.6 us  [the longest x1 83.1 us: layer_call(): pl.pallas_call(layer_kernel, out_shape=(S(wide, bf), S(flat, bf), S(flat,...]
    mul x1 -> x0, other arithmetic: 6.93 us -> none  [per_device(): weight_grad = total.astype(jnp.float32) * (1.0 / math.sqrt(65536))]
    unnamed x12 -> x0, local copies, waits for them, and re-layouts: 4.85 us -> none
where the time goes in v1:
time: 92.5 us; the launch traced here: 92.4 us
  Pallas kernels  91.6 us (99%)
    pallas_call x1, Pallas kernels, layer_call(): pl.pallas_call(layer_kernel, out_shape=(S(wide, bf), S(flat, bf), S(flat,...  83.1 us
    pallas_call x1, Pallas kernels, finish_call(): pl.pallas_call(kernel, out_shape=(S((1024, 2048), jnp.float32), S((TOK, 2...  8.5 us

profile of v1, /device:TPU:1, one launch (start us, length us, event | category | flops | bytes accessed | tf_op | source)
XLA Modules:
  0.0 92.4 jit_solution(13455556136352320822)
XLA Ops:
  0.6 83.1 %shard_map.101 = (bf16[512,2048]{1,0:T(8,128)(2,1)}, bf16[512,1024]{1,0:T(8,128)(2,1)}, bf16[512,1024]{1,0:T(8,128)(2,1)}, bf16[512,1024]{1,0:T(8,128)(2,1)}, bf16[1024,2048]{1,0:T(8,128)(2,1)}) custom-call(s32[8]{0:T(128)} %off_ref.1, bf16[512,1024]{1,0:T(8,128)(2,1)} %bitcast.9, bf16[512,1024]{1,0:T(8,128)(2,1)} %bitcast.10, bf16[512,1024]{1,0:T(8,128)(2,1)} %bitcast.11, ...), custom_call_target="tpu_custom_call" | custom-call | tf_op jit(solution)/shard_map/pallas_call | solution.py:399
  83.7 8.5 %shard_map.102 = (f32[1024,2048]{1,0:T(8,128)}, bf16[512,2048]{1,0:T(8,128)(2,1)}, bf16[512,1024]{1,0:T(8,128)(2,1)}, bf16[512,1024]{1,0:T(8,128)(2,1)}, bf16[512,1024]{1,0:T(8,128)(2,1)}) custom-call(bf16[1024,2048]{1,0:T(8,128)(2,1)} %get-tuple-element.15.refs_0_, bf16[512,2048]{1,0:T(8,128)(2,1)} %get-tuple-element.16.refs_1_, ...), custom_call_target="tpu_custom_call" | custom-call | tf_op jit(solution)/shard_map/pallas_call | solution.py:456

commit v2 on v1

--- a/solution.py
+++ b/solution.py
@@ -27,6 +27,8 @@
 
 
 def head_cols(h):
+    if isinstance(h, int):
+        return slice(h * DIM, h * DIM + DIM)
     return pl.ds(pl.multiple_of(h * DIM, DIM), DIM)
 
 
@@ -58,6 +60,8 @@
 STARTS = (0, 384, 768, 1152, 1536, 1792)
 COLS = [slice(a, a + b) for a, b in zip(STARTS, WIDTHS)]
 ORDERS = ((0, 1, 2), (1, 2, 0), (2, 0, 1)) * 2
+FAR_FIRST = sorted(((a, b, c) for a in range(4) for b in range(4) for c in range(4) if a + b + c > 0),
+                   key=lambda o: -sum(min(d, 4 - d) for d in o))
 
 
 def layer_kernel(off_ref, q_hbm, k_hbm, v_hbm, w_hbm, grad_hbm,
@@ -80,9 +84,10 @@
         load.start()
     pl.semaphore_signal(barrier, inc=1, device_id=sibling, device_id_type=MESH)
 
-    @pl.loop(1, 64)
-    def _(i):
-        pl.semaphore_signal(barrier, inc=1, device_id=(dp, lax.rem(seq + i, 64)), device_id_type=MESH)
+    moved = [[lax.rem(coord[axis] + d, 4) * STRIDES[axis] for d in range(4)] for axis in range(3)]
+    others = [moved[0][a] + moved[1][b] + moved[2][c] for a, b, c in FAR_FIRST]
+    for d in others:
+        pl.semaphore_signal(barrier, inc=1, device_id=(dp, d), device_id_type=MESH)
 
     started = []
     stores = []
@@ -104,17 +109,14 @@
     loads[0].wait()
     loads[1].wait()
 
-    @pl.loop(0, HEADS)
-    def _(h):
+    for h in range(HEADS):
         s = picker(off_ref[h]).astype(jnp.bfloat16)
         kv_sel[h, 0] = mm(s, k_ref[:, head_cols(h)]).astype(jnp.bfloat16)
         kv_sel[h, 1] = mm(s, v_ref[:, head_cols(h)]).astype(jnp.bfloat16)
 
     pl.semaphore_wait(barrier, 64)
 
-    @pl.loop(1, 64)
-    def _(i):
-        d = lax.rem(seq + i, 64)
+    for d in others:
         pltpu.make_async_remote_copy(
             src_ref=kv_sel.at[d // HOLD], dst_ref=kv_all.at[:, seq], send_sem=far_send.at[0], recv_sem=far_recv.at[0],
             device_id=(dp, d), device_id_type=MESH).start()
@@ -123,15 +125,13 @@
 
     loads[2].wait()
 
-    @pl.loop(0, HEADS)
-    def _(h):
+    for h in range(HEADS):
         s = picker(off_ref[h]).astype(jnp.bfloat16)
         q_sel[h] = mm(s, q_ref[:, head_cols(h)]).astype(jnp.bfloat16)
 
     to_group(q_sel, q_all, 1)
 
-    @pl.loop(0, HEADS)
-    def _(h):
+    for h in range(HEADS):
         o, lse = softmax_out(q_sel[h], k_ref[:, head_cols(h)], with_ones(v_ref[:, head_cols(h)]))
         os_sel[h, 0] = o
         os_sel[h, 1] = lse
@@ -146,8 +146,7 @@
         cols = pl.ds(pl.multiple_of(c * 256, 256), 256)
         g_ref[:, cols] = mm(grad_ref[...], w_ref[cols, :], NT).astype(jnp.bfloat16)
 
-    @pl.loop(0, HEADS)
-    def _(h):
+    for h in range(HEADS):
         s = picker(off_ref[h]).astype(jnp.bfloat16)
         g_sel[h] = mm(s, g_ref[:, head_cols(h)]).astype(jnp.bfloat16)
 
@@ -194,8 +193,7 @@
     delta_lane = stat_t[64:65, :]
     dq_acc[...] = jnp.zeros_like(dq_acc)
 
-    @pl.loop(0, 4)
-    def _(c):
+    for c in range(4):
         blocks = pl.ds(c * 16, 16)
         kc = kv_all[0, blocks].reshape(512, DIM)
         vc = kv_all[1, blocks].reshape(512, DIM)
@@ -209,9 +207,7 @@
 
     dqf[...] = (dq_acc[...] * SCALE).astype(jnp.bfloat16).reshape(HOLD, PICK, DIM)
 
-    @pl.loop(1, 64)
-    def _(i):
-        d = lax.rem(seq + i, 64)
+    for d in others:
         pltpu.make_async_remote_copy(
             src_ref=dkv.at[:, d], dst_ref=got_dkv.at[seq], send_sem=far_send.at[6], recv_sem=far_recv.at[6],
             device_id=(dp, d), device_id_type=MESH).start()
@@ -221,10 +217,14 @@
 
     wait_bytes(got_att.at[pl.ds(0, 7)], far_recv.at[4])
     lane1 = lax.rem(lax.broadcasted_iota(jnp.int32, (1, TOK), 1), RATE)
-    for h in range(HEADS):
-        rows = slice(h * DIM, h * DIM + DIM)
-        put = mm(got_att[h], picker(off_ref[h]).astype(jnp.bfloat16), TN)
-        near_t[rows, :] = jnp.where(lane1 == off_ref[h], put, near_t[rows, :].astype(jnp.float32)).astype(jnp.bfloat16)
+    def assemble(core):
+        for i in range(4):
+            h = core * 4 + i
+            rows = pl.ds(pl.multiple_of(h * DIM, DIM), DIM)
+            put = mm(got_att[h], picker(off_ref[h]).astype(jnp.bfloat16), TN)
+            near_t[rows, :] = jnp.where(lane1 == off_ref[h], put, near_t[rows, :].astype(jnp.float32)).astype(jnp.bfloat16)
+
+    assemble(1 - dp)
 
     def peer(axis, d):
         c = lax.rem(coord[axis] + d, 4)
@@ -244,8 +244,7 @@
     for p in range(6):
         s0[:, COLS[p]] = mm(near_t[pl.ds(other, 512), :], grad_ref[:, COLS[p]]).astype(jnp.bfloat16)
         first.append(copy(p, 0, s0.at[:, COLS[p]], r0.at[:, COLS[p]], sibling))
-    for p in range(6):
-        acc[:, COLS[p]] = mm(near_t[pl.ds(mine, 512), :], grad_ref[:, COLS[p]])
+    assemble(dp)
 
     flight = [None] * 6
 
@@ -261,7 +260,7 @@
     base1 = []
     for p in range(6):
         first[p].wait_recv()
-        acc[:, COLS[p]] += r0[:, COLS[p]].astype(jnp.float32)
+        acc[:, COLS[p]] = mm(near_t[pl.ds(mine, 512), :], grad_ref[:, COLS[p]]) + r0[:, COLS[p]].astype(jnp.float32)
         send_rows(p, 0, 0, 128, sbuf, rbuf1)
         base1.append(pl.multiple_of(coord[ORDERS[p][0]] * 128, 128))
 

time: 92.5 us -> 89.1 us (0.963)
  Pallas kernels: 91.6 us -> 88.2 us
    pallas_call x1, Pallas kernels: 83.1 us -> 79.7 us  [layer_call(): pl.pallas_call(layer_kernel, out_shape=(S(wide, bf), S(flat, bf), S(flat,...]
where the time goes in v2:
time: 89.1 us; the launch traced here: 89 us
  Pallas kernels  88.2 us (99%)
    pallas_call x1, Pallas kernels, layer_call(): pl.pallas_call(layer_kernel, out_shape=(S(wide, bf), S(flat, bf), S(flat,...  79.7 us
    pallas_call x1, Pallas kernels, finish_call(): pl.pallas_call(kernel, out_shape=(S((1024, 2048), jnp.float32), S((TOK, 2...  8.5 us

profile of v2, /device:TPU:1, one launch (start us, length us, event | category | flops | bytes accessed | tf_op | source)
XLA Modules:
  0.0 89.0 jit_solution(15723502514536250017)
XLA Ops:
  0.6 79.7 %shard_map.101 = (bf16[512,2048]{1,0:T(8,128)(2,1)}, bf16[512,1024]{1,0:T(8,128)(2,1)}, bf16[512,1024]{1,0:T(8,128)(2,1)}, bf16[512,1024]{1,0:T(8,128)(2,1)}, bf16[1024,2048]{1,0:T(8,128)(2,1)}) custom-call(s32[8]{0:T(128)} %off_ref.1, bf16[512,1024]{1,0:T(8,128)(2,1)} %bitcast.9, bf16[512,1024]{1,0:T(8,128)(2,1)} %bitcast.10, bf16[512,1024]{1,0:T(8,128)(2,1)} %bitcast.11, ...), custom_call_target="tpu_custom_call" | custom-call | tf_op jit(solution)/shard_map/pallas_call | solution.py:398
  80.3 8.5 %shard_map.102 = (f32[1024,2048]{1,0:T(8,128)}, bf16[512,2048]{1,0:T(8,128)(2,1)}, bf16[512,1024]{1,0:T(8,128)(2,1)}, bf16[512,1024]{1,0:T(8,128)(2,1)}, bf16[512,1024]{1,0:T(8,128)(2,1)}) custom-call(bf16[1024,2048]{1,0:T(8,128)(2,1)} %get-tuple-element.15.refs_0_, bf16[512,2048]{1,0:T(8,128)(2,1)} %get-tuple-element.16.refs_1_, ...), custom_call_target="tpu_custom_call" | custom-call | tf_op jit(solution)/shard_map/pallas_call | solution.py:455

commit v3 on v2

--- a/solution.py
+++ b/solution.py
@@ -49,6 +49,18 @@
     ov = mm(e, v1)
     total = ov[:, DIM:]
     return ov[:, :DIM] / total, top + jnp.log(total) * LOG2E
+
+
+def split3(x):
+    high = x.astype(jnp.bfloat16).astype(jnp.float32)
+    mid = (x - high).astype(jnp.bfloat16).astype(jnp.float32)
+    lane = lax.broadcasted_iota(jnp.int32, x.shape, 1)
+    return jnp.where(lane < 32, high, jnp.where(lane < 64, mid, x - high - mid)).astype(jnp.bfloat16)
+
+
+def join3(code, at):
+    x = code.astype(jnp.float32)
+    return x[:, at:at + 1] + x[:, at + 32:at + 33] + x[:, at + 64:at + 65]
 
 
 def wait_bytes(ref, sem):
@@ -133,8 +145,8 @@
 
     for h in range(HEADS):
         o, lse = softmax_out(q_sel[h], k_ref[:, head_cols(h)], with_ones(v_ref[:, head_cols(h)]))
-        os_sel[h, 0] = o
-        os_sel[h, 1] = lse
+        os_sel[h, 0] = o.astype(jnp.bfloat16)
+        os_sel[h, 1] = split3(lse)
 
     to_group(os_sel, os_all, 2)
 
@@ -174,8 +186,8 @@
     far_out = jnp.concatenate([f[0] for f in far], axis=0)
     far_lse = jnp.concatenate([f[1] for f in far], axis=0)
     wait_bytes(os_all.at[pl.ds(0, 7)], far_recv.at[2])
-    near_sel = os_all[:, 0].reshape(256, DIM)
-    near_lse = os_all[:, 1].reshape(256, DIM)
+    near_sel = os_all[:, 0].reshape(256, DIM).astype(jnp.float32)
+    near_lse = join3(os_all[:, 1].reshape(256, DIM), 0)
     top = jnp.maximum(near_lse, far_lse)
     mixed = top + jnp.log(jnp.exp2(near_lse - top) + jnp.exp2(far_lse - top)) * LOG2E
     att = (jnp.exp2(near_lse - mixed) * near_sel + jnp.exp2(far_lse - mixed) * far_out).astype(jnp.bfloat16)
@@ -186,7 +198,7 @@
     delta = jnp.sum(g.astype(jnp.float32) * att.astype(jnp.float32), axis=1, keepdims=True)
     lane = lax.broadcasted_iota(jnp.int32, (256, DIM), 1)
     stat = jnp.where(lane < 64, mixed, delta)
-    back_stat[...] = stat.reshape(HOLD, PICK, DIM)
+    back_stat[...] = split3(jnp.where(lax.rem(lane, 32) < 16, mixed, delta)).reshape(HOLD, PICK, DIM)
     to_group(back_stat, got_stat, 5)
     stat_t = stat.T
     mixed_lane = stat_t[0:1, :]
@@ -270,9 +282,9 @@
         for h in range(HEADS):
             pick = picker(off_ref[h])
             st = got_stat[h]
-            mixed_h = jnp.sum(jnp.where(pick, st[:, 0:1], 0.0), axis=0, keepdims=True)
+            mixed_h = jnp.sum(jnp.where(pick, join3(st, 0), 0.0), axis=0, keepdims=True)
             lse_ref[h:h + 1, :] = jnp.where(lane1 == off_ref[h], mixed_h, lse_ref[h:h + 1, :])
-            delta_ref[h:h + 1, :] = jnp.sum(jnp.where(pick, st[:, 64:65], 0.0), axis=0, keepdims=True)
+            delta_ref[h:h + 1, :] = jnp.sum(jnp.where(pick, join3(st, 16), 0.0), axis=0, keepdims=True)
 
     def project(c):
         cs = slice(c * 512, c * 512 + 512)
@@ -403,9 +415,9 @@
         scratch_shapes=[
             V(flat, bf), V(flat, bf), V(flat, bf), V((1024, 2048), bf), V(wide, bf), V(flat, bf), V(flat, bf),
             V(wide, bf), V(flat, bf), V(flat, bf), V(flat, bf),
-            V((HEADS, 2, PICK, DIM), bf), V(rows, bf), V(rows, bf), V((HEADS, 2, PICK, DIM), f32),
-            V((2, 64, PICK, DIM), bf), V(rows, bf), V(rows, bf), V((HOLD, 2, PICK, DIM), f32),
-            V(rows, bf), V(rows, f32), V(rows, bf), V(rows, f32),
+            V((HEADS, 2, PICK, DIM), bf), V(rows, bf), V(rows, bf), V((HEADS, 2, PICK, DIM), bf),
+            V((2, 64, PICK, DIM), bf), V(rows, bf), V(rows, bf), V((HOLD, 2, PICK, DIM), bf),
+            V(rows, bf), V(rows, bf), V(rows, bf), V(rows, bf),
             V((2, 64, PICK, DIM), bf), V(rows, bf), V((64, 2, PICK, DIM), bf), V(rows, bf),
             V((1024, TOK), bf), V((TOK, 128), f32), V((HEADS, TOK), f32), V((HEADS, TOK), f32), V((256, DIM), f32),
             V(flat, f32), V(flat, f32), V(flat, f32),

time: 89.1 us -> 87.6 us (0.983)
  Pallas kernels: 88.2 us -> 86.6 us
    pallas_call x1, Pallas kernels: 79.7 us -> 78.1 us  [layer_call(): pl.pallas_call(layer_kernel, out_shape=(S(wide, bf), S(flat, bf), S(flat,...]
where the time goes in v3:
time: 87.6 us; the launch traced here: 87.5 us
  Pallas kernels  86.6 us (99%)
    pallas_call x1, Pallas kernels, layer_call(): pl.pallas_call(layer_kernel, out_shape=(S(wide, bf), S(flat, bf), S(flat,...  78.1 us
    pallas_call x1, Pallas kernels, finish_call(): pl.pallas_call(kernel, out_shape=(S((1024, 2048), jnp.float32), S((TOK, 2...  8.5 us

profile of v3, /device:TPU:1, one launch (start us, length us, event | category | flops | bytes accessed | tf_op | source)
XLA Modules:
  0.0 87.5 jit_solution(10201105754787210643)
XLA Ops:
  0.6 78.1 %shard_map.101 = (bf16[512,2048]{1,0:T(8,128)(2,1)}, bf16[512,1024]{1,0:T(8,128)(2,1)}, bf16[512,1024]{1,0:T(8,128)(2,1)}, bf16[512,1024]{1,0:T(8,128)(2,1)}, bf16[1024,2048]{1,0:T(8,128)(2,1)}) custom-call(s32[8]{0:T(128)} %off_ref.1, bf16[512,1024]{1,0:T(8,128)(2,1)} %bitcast.9, bf16[512,1024]{1,0:T(8,128)(2,1)} %bitcast.10, bf16[512,1024]{1,0:T(8,128)(2,1)} %bitcast.11, ...), custom_call_target="tpu_custom_call" | custom-call | tf_op jit(solution)/shard_map/pallas_call | solution.py:410
  78.8 8.5 %shard_map.102 = (f32[1024,2048]{1,0:T(8,128)}, bf16[512,2048]{1,0:T(8,128)(2,1)}, bf16[512,1024]{1,0:T(8,128)(2,1)}, bf16[512,1024]{1,0:T(8,128)(2,1)}, bf16[512,1024]{1,0:T(8,128)(2,1)}) custom-call(bf16[1024,2048]{1,0:T(8,128)(2,1)} %get-tuple-element.15.refs_0_, bf16[512,2048]{1,0:T(8,128)(2,1)} %get-tuple-element.16.refs_1_, ...), custom_call_target="tpu_custom_call" | custom-call | tf_op jit(solution)/shard_map/pallas_call | solution.py:467
